TPU v7x, 32 devices: a whole 2x2x4 slice. The times are simulated.
32 devices in a mesh: rows: 4 (over y, x), cols: 8 (over z, core).
Axes of the slice: x: 2, y: 2, z: 4, core: 2. Of those that a mesh axis runs over, the one named last changes fastest.
Arguments:
- design: float32 [6, 8, 64], P(None, 'rows', 'cols'), may hold values from -6 to 6
- active: int32 [8, 64], P('rows', 'cols'), may hold values 0 or 1
- stamp_basis: float32 [6, 32, 32], replicated, may hold values from -2 to 2
- film_field: bfloat16 [16, 128, 1024], P(None, 'rows', 'cols'), may hold values from -6 to 6
- lift_weight: float32 [16], replicated, may hold values from -4 to 4
- lift_bias: float32 [16], replicated, may hold values from -3 to 3
- conv_weight: bfloat16 [4, 9, 16, 16], replicated, may hold values from -0.5 to 0.5
- conv_bias: float32 [4, 16], replicated, may hold values from -3 to 3
- readout: float32 [16], replicated, may hold values from -1.5 to 1.5
- target: float32 [128, 1024], P('rows', 'cols'), may hold values from -6 to 6
- dilation: int32 [4], replicated, may hold values from 1 to 8, as said below
Outputs:
- new_design: float32 [6, 8, 64], P(None, 'rows', 'cols')
- objective: float32 [2], replicated
Inputs may be any that keep to these rules, and one draw needn't show every extreme that they name: The dilation of each layer is an integer from 1 to 8; some layer has exactly 8.
All inputs are finite; a program needn't handle non-finite values. No bound on the sum of `active` on one device may be relied on, other than what follows from the above.
Results may differ from a plain program's by a relative error of at most 0.0025.
Values may be sent and summed in bfloat16 or wider, within the bound.
A program may use at most 64 MiB of HBM per device.

v0:
```python
import functools

import jax
import jax.numpy as jnp
import numpy as np
from jax import lax
from jax.experimental import pallas as pl
from jax.experimental.pallas import tpu as pltpu
from jax.sharding import PartitionSpec as P

DMAX = 8
LAYERS = 4
ITERS = 2
LANES = 128

step_rate = 0.25
norm_eps = 1e-06

MESH = pl.DeviceIdType.MESH
F32 = jnp.float32
BF16 = jnp.bfloat16
OTHERS = [0, 1, 2, 3, 5, 6, 7, 8]
PER_ITER = 2 * LAYERS + 2


def tap_list():
    return [(row_step, col_step) for row_step in (-1, 0, 1) for col_step in (-1, 0, 1)]


def split3(value):
    high = value.astype(BF16)
    rest = value - high.astype(F32)
    mid = rest.astype(BF16)
    low = (rest - mid.astype(F32)).astype(BF16)
    return high, mid, low


def exact_dot(a, b):
    return jnp.dot(a, b, precision=lax.Precision.HIGHEST, preferred_element_type=F32)


def exact_dot_nt(a, b):
    return lax.dot_general(
        a, b, (((1,), (1,)), ((), ())), precision=lax.Precision.HIGHEST, preferred_element_type=F32
    )


def kernel(
    cfg,
    dil_ref, design_ref, active_ref, film_ref, target_ref, lanes_ref, wt_ref, blk_ref, sel_ref, selt_ref,
    new_ref, obj_ref,
    center, halo_l, halo_r, edge_l, edge_r, state_s, x_s, wbig, pre_s, adj_s, ee_s,
    amp9, part, got, grad9, q_s, grad_t, ar, ar_src,
    send_sem, recv_sem, ar_send, ar_recv,
):
    nrow, ncol, rows, total_cells, total_entries = cfg
    ndev = nrow * ncol
    nx = rows * 16
    my_r = lax.axis_index("rows")
    my_c = lax.axis_index("cols")
    me = my_r * ncol + my_c

    def exists(m):
        dr, dc = m // 3 - 1, m % 3 - 1
        r, c = my_r + dr, my_c + dc
        return (r >= 0) & (r < nrow) & (c >= 0) & (c < ncol)

    def ident(m):
        dr, dc = m // 3 - 1, m % 3 - 1
        return (my_r + dr, my_c + dc)

    def desc(phase, m, src, dst):
        return pltpu.make_async_remote_copy(
            src_ref=src(m), dst_ref=dst(m),
            send_sem=send_sem.at[phase, m], recv_sem=recv_sem.at[phase, m],
            device_id=ident(m), device_id_type=MESH,
        )

    def start(phase, src, dst):
        for m in OTHERS:
            @pl.when(exists(m))
            def _():
                desc(phase, m, src, dst).start()

    def arrive(phase, src, dst):
        for m in OTHERS:
            @pl.when(exists(8 - m))
            def _():
                desc(phase, m, src, dst).wait_recv()

    def sent(phase, src, dst):
        for m in OTHERS:
            @pl.when(exists(m))
            def _():
                desc(phase, m, src, dst).wait_send()

    def state_refs(slot):
        c = center.at[slot]
        el, er, hl, hr = edge_l.at[slot], edge_r.at[slot], halo_l.at[slot], halo_r.at[slot]
        D, R = DMAX, rows

        def src(m):
            return {
                0: lambda: el.at[pl.ds(0, D)], 1: lambda: c.at[pl.ds(D, D)], 2: lambda: er.at[pl.ds(0, D)],
                3: lambda: el, 5: lambda: er,
                6: lambda: el.at[pl.ds(R - D, D)], 7: lambda: c.at[pl.ds(R, D)], 8: lambda: er.at[pl.ds(R - D, D)],
            }[m]()

        def dst(m):
            return {
                0: lambda: hr.at[pl.ds(R + D, D)], 1: lambda: c.at[pl.ds(R + D, D)], 2: lambda: hl.at[pl.ds(R + D, D)],
                3: lambda: hr.at[pl.ds(D, R)], 5: lambda: hl.at[pl.ds(D, R)],
                6: lambda: hr.at[pl.ds(0, D)], 7: lambda: c.at[pl.ds(0, D)], 8: lambda: hl.at[pl.ds(0, D)],
            }[m]()

        return src, dst

    def amp_refs(_):
        return (lambda m: amp9.at[4]), (lambda m: amp9.at[8 - m])

    def part_refs(it):
        return (lambda m: part.at[it, m]), (lambda m: got.at[it, 8 - m])

    def grad_refs(it):
        return (lambda m: grad_t.at[it]), (lambda m: grad9.at[it, 8 - m])

    nslot = ITERS * 2 * LAYERS

    def clear(slot, _):
        z = jnp.zeros((DMAX, 16, LANES), BF16)
        center[slot, 0:DMAX] = z
        center[slot, rows + DMAX : rows + 2 * DMAX] = z
        zh = jnp.zeros((rows + 2 * DMAX, LANES), F32)
        halo_l[slot] = zh
        halo_r[slot] = zh
        return 0

    lax.fori_loop(0, nslot, clear, 0)
    z9 = jnp.zeros((9, 16, LANES), F32)
    amp9[...] = z9
    for it in range(ITERS):
        got[it] = z9
        grad9[it] = z9
    amp9[4] = design_ref[...] * active_ref[...]

    barrier = pltpu.get_barrier_semaphore()

    def greet(k, _):
        other = lax.rem(me + k, ndev)
        pl.semaphore_signal(barrier, inc=1, device_id=(other // ncol, lax.rem(other, ncol)), device_id_type=MESH)
        return 0

    lax.fori_loop(1, ndev, greet, 0)
    pl.semaphore_wait(barrier, ndev - 1)

    amp_phase = ITERS * PER_ITER
    start(amp_phase, *amp_refs(0))

    lane = lax.broadcasted_iota(jnp.int32, (24, 16, LANES), 2) // 16
    jpos = lax.broadcasted_iota(jnp.int32, (24, 16, LANES), 0) - 8 - lane
    for l in range(LAYERS):
        d = dil_ref[l]
        masks = [jpos == rx * d for rx in (-1, 0, 1)]
        for f in range(2):
            for ry in range(3):
                acc = jnp.zeros((24, 16, LANES), F32)
                for rx in range(3):
                    w = wt_ref[f, l, 3 * ry + rx].astype(F32)
                    acc = jnp.where(masks[rx], w[None], acc)
                wbig[f, l, ry] = acc.astype(BF16).reshape(384, LANES)
    ones_block = (
        lax.broadcasted_iota(jnp.int32, (LANES, LANES), 0) // 16
        == lax.broadcasted_iota(jnp.int32, (LANES, LANES), 1) // 16
    ).astype(F32).astype(BF16)
    pos = lax.broadcasted_iota(jnp.int32, (LANES, 16 * LANES), 0)
    col = lax.broadcasted_iota(jnp.int32, (LANES, 16 * LANES), 1)
    ee_s[...] = (pos == (col // LANES) * 8 + (col % LANES) // 16).astype(F32).astype(BF16)

    lw = lanes_ref[0:1, :]
    lb = lanes_ref[1:2, :]
    ro = lanes_ref[2:3, :]
    bsub = lax.broadcasted_iota(jnp.int32, (rows + 2 * DMAX, 8, LANES), 1)

    def publish(slot, phase, value):
        state_s[...] = value.reshape(rows, 16, LANES)
        center[slot, DMAX : rows + DMAX] = value.astype(BF16).reshape(rows, 16, LANES)
        edge_l[slot] = state_s[:, 0, :]
        edge_r[slot] = state_s[:, 15, :]
        start(phase, *state_refs(slot))

    def conv(slot, phase, f, l):
        arrive(phase, *state_refs(slot))
        cb = center[slot]
        c = cb.astype(F32)
        c0, c1 = c[:, 0:8], c[:, 8:16]
        hl = halo_l[slot][:, None, :]
        hr = halo_r[slot][:, None, :]
        l0 = jnp.where(bsub == 0, hl, pltpu.roll(c1, 1, 1))
        r1 = jnp.where(bsub == 7, hr, pltpu.roll(c0, 7, 1))
        x_s[:, :, 0:128] = jnp.concatenate([l0, c0], axis=1).astype(BF16)
        x_s[:, :, 128:256] = cb
        x_s[:, :, 256:384] = jnp.concatenate([c1, r1], axis=1).astype(BF16)
        d = dil_ref[l]
        out = None
        for ry in range(3):
            lhs = x_s[pl.ds(DMAX + (ry - 1) * d, rows)].reshape(nx, 384)
            term = jnp.dot(lhs, wbig[f, l, ry], preferred_element_type=F32)
            out = term if out is None else out + term
        return out

    def sigmoid(v):
        return 1.0 / (1.0 + jnp.exp(-v))

    arrive(amp_phase, *amp_refs(0))
    sent(amp_phase, *amp_refs(0))

    def step(it, _):
        base = it * PER_ITER
        slot0 = it * 2 * LAYERS
        picked = exact_dot(sel_ref[...], amp9[...].reshape(144, LANES))
        height = jnp.zeros((16, 256), F32)
        for t in range(9):
            height = height + exact_dot(picked[16 * t : 16 * t + 16, 0:8], blk_ref[t])
        two = jnp.concatenate([height[:, 0:128], height[:, 128:256]], axis=0)
        spread = None
        for piece in split3(two):
            term = jnp.dot(piece, ee_s[...], preferred_element_type=F32)
            spread = term if spread is None else spread + term
        for s in range(2):
            for k in range(16):
                q = 16 * s + k
                y, xh = q // 2, q % 2
                for a in range(rows // 16):
                    v = spread[16 * s + 8 * a : 16 * s + 8 * a + 8, 128 * k : 128 * k + 128]
                    state_s[16 * a + y, 8 * xh : 8 * xh + 8, :] = v
        h = state_s[...].reshape(nx, LANES)
        state = (lw * h + lb + film_ref[...].astype(F32).reshape(nx, LANES)).astype(BF16).astype(F32)
        for l in range(LAYERS):
            publish(slot0 + l, base + l, state)
            pre = conv(slot0 + l, base + l, 0, l) + lanes_ref[4 + l : 5 + l, :]
            pre_s[l] = pre
            state = (state + pre * sigmoid(pre)).astype(BF16).astype(F32)
        pressure = None
        for piece in split3(ro * state):
            term = jnp.dot(piece, ones_block, preferred_element_type=F32)
            pressure = term if pressure is None else pressure + term
        misfit = pressure - target_ref[...].reshape(nx, LANES)
        miss = jnp.sum(misfit * misfit, keepdims=True) * (0.5 / 16)
        adjoint = ro * (misfit * (1.0 / 256.0))
        for n in range(LAYERS):
            l = LAYERS - 1 - n
            v = pre_s[l]
            s = sigmoid(v)
            slope = (adjoint * (s * (1.0 + v * (1.0 - s)))).astype(BF16).astype(F32)
            publish(slot0 + LAYERS + n, base + LAYERS + n, slope)
            adjoint = adjoint + conv(slot0 + LAYERS + n, base + LAYERS + n, 1, l)
        adj_s[...] = (lw * adjoint).reshape(rows, 16, LANES)
        strips = []
        for s in range(2):
            tiles = []
            for k in range(16):
                q = 16 * s + k
                y, xh = q // 2, q % 2
                tiles.append(
                    jnp.concatenate(
                        [adj_s[16 * a + y, 8 * xh : 8 * xh + 8, :] for a in range(rows // 16)], axis=0
                    )
                )
            strips.append(jnp.concatenate(tiles, axis=1))
        both = jnp.concatenate(strips, axis=0)
        folded = None
        for piece in split3(both):
            term = lax.dot_general(
                piece, ee_s[...], (((1,), (1,)), ((), ())), preferred_element_type=F32
            )
            folded = term if folded is None else folded + term
        hg = jnp.concatenate([folded[0:16], folded[16:32]], axis=1)
        q_s[...] = jnp.zeros((144, LANES), F32)
        for t in range(9):
            q_s[16 * t : 16 * t + 16, 0:8] = exact_dot_nt(hg, blk_ref[t])
        mine = exact_dot(selt_ref[...], q_s[...]).reshape(9, 16, LANES)
        part[it] = mine
        p_phase = base + 2 * LAYERS
        start(p_phase, *part_refs(it))
        got[it, 4] = mine[4]
        arrive(p_phase, *part_refs(it))
        gradient = jnp.sum(got[it], axis=0) * active_ref[...]
        grad_t[it] = gradient
        squares = jnp.sum(gradient * gradient, keepdims=True)
        sub = lax.broadcasted_iota(jnp.int32, (8, LANES), 0)
        tile = jnp.where(sub == 0, squares, miss)
        ar_src[it] = tile
        g_phase = p_phase + 1

        def tell(k, _):
            other = lax.rem(me + k, ndev)
            pltpu.make_async_remote_copy(
                src_ref=ar_src.at[it], dst_ref=ar.at[it, me],
                send_sem=ar_send.at[it], recv_sem=ar_recv.at[it],
                device_id=(other // ncol, lax.rem(other, ncol)), device_id_type=MESH,
            ).start()
            return 0

        lax.fori_loop(1, ndev, tell, 0)
        start(g_phase, *grad_refs(it))
        ar[it, me] = tile
        many = ar.at[it, pl.ds(0, ndev - 1)]
        pltpu.make_async_copy(many, many, ar_recv.at[it]).wait()
        arrive(g_phase, *grad_refs(it))
        total = jnp.sum(ar[it], axis=0)
        scale = step_rate / jnp.sqrt(total[0:1] * (1.0 / total_entries) + norm_eps)
        obj_ref[it] = total * (1.0 / total_cells)
        grad9[it, 4] = gradient
        amp9[...] = amp9[...] - grad9[it] * scale[None]
        new_ref[...] = new_ref[...] - gradient * scale
        return 0

    new_ref[...] = design_ref[...]
    lax.fori_loop(0, ITERS, step, 0)

    def drain(it, _):
        base = it * PER_ITER
        for n in range(2 * LAYERS):
            sent(base + n, *state_refs(it * 2 * LAYERS + n))
        sent(base + 2 * LAYERS, *part_refs(it))
        sent(base + 2 * LAYERS + 1, *grad_refs(it))
        many = ar.at[it, pl.ds(0, ndev - 1)]
        pltpu.make_async_copy(many, many, ar_send.at[it]).wait()
        return 0

    lax.fori_loop(0, ITERS, drain, 0)


def select_matrix(dr_count, dc_count):
    sel = np.zeros((9, dr_count, dc_count, 9, dr_count, dc_count), np.float32)
    for t, (ry, rx) in enumerate(tap_list()):
        for a in range(dr_count):
            for b in range(dc_count):
                ta, tb = a + ry, b + rx
                nr, nc = ta // dr_count, tb // dc_count
                sel[t, a, b, 3 * (nr + 1) + nc + 1, ta - nr * dr_count, tb - nc * dc_count] = 1
    size = 9 * dr_count * dc_count
    return sel.reshape(size, size)


def basis_blocks(stamp_basis):
    side = stamp_basis.shape[1] // 2
    padded_basis = jnp.pad(stamp_basis, ((0, 0), (side, side), (side, side)))
    pieces = []
    for row_step, col_step in tap_list():
        top = side + side // 2 - side * row_step
        left = side + side // 2 - side * col_step
        pieces.append(padded_basis[:, top : top + side, left : left + side])
    return jnp.stack(pieces)


def on_device(
    design, active, stamp_basis, film_field, lift_weight, lift_bias, conv_weight, conv_bias, readout, target, dilation
):
    channels, rows, cols = film_field.shape
    nparams, drows, dcols = design.shape
    nrow = lax.axis_size("rows")
    ncol = lax.axis_size("cols")
    ndev = nrow * ncol
    total_cells = rows * cols * ndev
    total_entries = nparams * drows * dcols * ndev

    def by_dimple(v):
        v = v.reshape(nparams, drows * dcols).T
        return jnp.pad(v, ((0, 0), (0, LANES - nparams)))

    design_t = by_dimple(design)
    active_t = jnp.broadcast_to(active.astype(F32).reshape(drows * dcols, 1), (drows * dcols, LANES))
    film = film_field.reshape(channels, rows, dcols, 2, 8).transpose(1, 3, 2, 4, 0).reshape(rows, 16, LANES)
    targ = target.reshape(rows, dcols, 2, 8).transpose(0, 2, 1, 3).reshape(rows, 16, 8, 1)
    targ = jnp.broadcast_to(targ, (rows, 16, 8, 16)).reshape(rows, 16, LANES)
    lanes = jnp.concatenate(
        [jnp.tile(jnp.stack([lift_weight, lift_bias, readout, readout]), (1, 8)), jnp.tile(conv_bias, (1, 8))]
    )
    wt = jnp.stack([jnp.swapaxes(conv_weight, 2, 3), conv_weight[:, ::-1]])
    wt = jnp.tile(wt, (1, 1, 1, 1, 8))
    blocks = jnp.pad(basis_blocks(stamp_basis), ((0, 0), (0, 8 - nparams), (0, 0), (0, 0))).reshape(9, 8, 256)
    sel = select_matrix(drows, dcols)

    nslot = ITERS * 2 * LAYERS
    phases = ITERS * PER_ITER + 1
    tall = rows + 2 * DMAX
    vmem = pl.BlockSpec(memory_space=pltpu.VMEM)
    new, obj = pl.pallas_call(
        functools.partial(kernel, (nrow, ncol, rows, total_cells, total_entries)),
        out_shape=(
            jax.ShapeDtypeStruct((16, LANES), F32),
            jax.ShapeDtypeStruct((ITERS, 8, LANES), F32),
        ),
        in_specs=[pl.BlockSpec(memory_space=pltpu.SMEM)] + [vmem] * 9,
        out_specs=(vmem, vmem),
        scratch_shapes=[
            pltpu.VMEM((nslot, tall, 16, LANES), BF16),
            pltpu.VMEM((nslot, tall, LANES), F32),
            pltpu.VMEM((nslot, tall, LANES), F32),
            pltpu.VMEM((nslot, rows, LANES), F32),
            pltpu.VMEM((nslot, rows, LANES), F32),
            pltpu.VMEM((rows, 16, LANES), F32),
            pltpu.VMEM((tall, 16, 384), BF16),
            pltpu.VMEM((2, LAYERS, 3, 384, LANES), BF16),
            pltpu.VMEM((LAYERS, rows * 16, LANES), F32),
            pltpu.VMEM((rows, 16, LANES), F32),
            pltpu.VMEM((LANES, 16 * LANES), BF16),
            pltpu.VMEM((9, 16, LANES), F32),
            pltpu.VMEM((ITERS, 9, 16, LANES), F32),
            pltpu.VMEM((ITERS, 9, 16, LANES), F32),
            pltpu.VMEM((ITERS, 9, 16, LANES), F32),
            pltpu.VMEM((144, LANES), F32),
            pltpu.VMEM((ITERS, 16, LANES), F32),
            pltpu.VMEM((ITERS, ndev, 8, LANES), F32),
            pltpu.VMEM((ITERS, 8, LANES), F32),
            pltpu.SemaphoreType.DMA((phases, 9)),
            pltpu.SemaphoreType.DMA((phases, 9)),
            pltpu.SemaphoreType.DMA((ITERS,)),
            pltpu.SemaphoreType.DMA((ITERS,)),
        ],
        compiler_params=pltpu.CompilerParams(
            collective_id=0, has_side_effects=True, vmem_limit_bytes=40 * 1024 * 1024
        ),
    )(dilation, design_t, active_t, film, targ, lanes, wt, blocks, sel, sel.T)
    new_design = new[:, :nparams].T.reshape(nparams, drows, dcols)
    return new_design, obj[:, 1, 0]


def solution(mesh):
    placed = (
        P(None, "rows", "cols"),
        P("rows", "cols"),
        P(),
        P(None, "rows", "cols"),
        P(),
        P(),
        P(),
        P(),
        P(),
        P("rows", "cols"),
        P(),
    )
    return jax.shard_map(
        on_device,
        mesh=mesh,
        in_specs=placed,
        out_specs=(P(None, "rows", "cols"), P()),
        check_vma=False,
    )
```

profile of v0, /device:TPU:0, one launch (start us, length us, event | category | flops | bytes accessed | tf_op | source)
XLA Modules:
  0.0 125.5 jit_solution(12584862037528988290)
XLA Ops:
  0.6 0.9 fusion.1
  1.5 0.8 fusion.3
  2.3 0.8 fusion.5
  3.1 0.9 fusion.7
  4.0 0.9 bitcast_dynamic-update-slice_fusion
  4.9 0.9 fusion.9
  5.8 0.8 fusion.11
  6.6 0.8 fusion.13
  7.4 0.8 fusion.15
  8.3 0.3 reshape.46.blk_ref
  8.5 0.1 copy.24
  8.7 0.1 pad_maximum_fusion
  8.8 0.6 tile.31
  9.4 0.0 copy-start.4
  9.4 1.6 %tile.32.wt_ref = bf16[2,4,9,16,128]{4,3,2,1,0:T(8,128)(2,1)S(1)} reshape(bf16[2,4,9,16,8,16]{5,4,3,2,1,0:T(8,128)(2,1)S(1)} %tile.31) | data formatting | bytes 589824 | tf_op jit(solution)/shard_map/tile | solution.py:381
  11.0 0.1 copy.22
  11.1 0.0 copy-start.10
  11.2 0.0 copy-start
  11.2 0.0 copy-start.1
  11.2 0.1 broadcast_in_dim.17
  11.3 0.3 copy.26.target_ref
  11.6 0.3 copy.20
  11.9 0.3 copy.21
  12.3 0.2 copy.25.film_ref
  12.6 0.1 tile.13
  12.7 0.1 tile.30
  12.8 0.1 copy.28
  12.9 0.1 broadcast_in_dim.14
  13.0 0.1 broadcast_in_dim.15.active_ref
  13.0 111.1 %shard_map.140 = (f32[16,128]{1,0:T(8,128)S(1)}, f32[2,8,128]{2,1,0:T(8,128)S(1)}) custom-call(s32[4]{0:T(128)S(1)} %copy-done.2, f32[16,128]{1,0:T(8,128)S(1)} %pad.12.design_ref, f32[16,128]{1,0:T(8,128)S(1)} %broadcast_in_dim.15.active_ref, bf16[32,16,128]{2,1,0:T(8,128)(2,1)S(1)} %copy.25.film_ref, f32[32,16,128]{2,1,0:T(8,128)S(1)} %copy.26.target_ref, ...), custom_call_target="tpu_custom_call" | custom-call | tf_op jit(solution)/shard_map/pallas_call | solution.py:389
  124.2 0.7 copy.29
  124.9 0.6 slice_reduce_fusion
  (30 shorter events, 0.2 us)
Async XLA Ops:
  0.6 7.9 %copy-start.3 = (bf16[4,9,16,16]{3,2,1,0:T(8,128)(2,1)S(1)}, bf16[4,9,16,16]{3,2,1,0:T(8,128)(2,1)}, u32[]{:S(2)}) copy-start(bf16[4,9,16,16]{3,2,1,0:T(8,128)(2,1)} %param.19) | copy-start | bytes 55300
  8.8 2.2 %copy-start.5 = (f32[32,128]{1,0:T(8,128)S(1)}, f32[32,128]{1,0:T(8,128)}, u32[]{:S(2)}) copy-start(f32[32,128]{1,0:T(8,128)} %param.22) | copy-start | bytes 49156
  9.4 2.2 %copy-start.4 = (bf16[16,32,128]{2,1,0:T(8,128)(2,1)S(1)}, bf16[16,32,128]{2,1,0:T(8,128)(2,1)}, u32[]{:S(2)}) copy-start(bf16[16,32,128]{2,1,0:T(8,128)(2,1)} %param.16) | copy-start | bytes 393220
  11.1 1.4 %copy-start.9 = (f32[16]{0:T(128)S(1)}, f32[16]{0:T(128)}, u32[]{:S(2)}) copy-start(f32[16]{0:T(128)} %param.21) | copy-start | bytes 196
  11.1 1.4 %copy-start.10 = (f32[16]{0:T(128)S(1)}, f32[16]{0:T(128)}, u32[]{:S(2)}) copy-start(f32[16]{0:T(128)} %param.18) | copy-start | bytes 196
  11.1 1.4 %copy-start.11 = (f32[16]{0:T(128)S(1)}, f32[16]{0:T(128)}, u32[]{:S(2)}) copy-start(f32[16]{0:T(128)} %param.17) | copy-start | bytes 196
  11.1 1.5 %copy-start.7 = (f32[4,16]{1,0:T(4,128)S(1)}, f32[4,16]{1,0:T(4,128)}, u32[]{:S(2)}) copy-start(f32[4,16]{1,0:T(4,128)} %param.20) | copy-start | bytes 772
  11.2 1.6 %copy-start.6 = (f32[6,2,8]{2,1,0:T(2,128)S(1)}, f32[6,2,8]{2,1,0:T(2,128)}, u32[]{:S(2)}) copy-start(f32[6,2,8]{2,1,0:T(2,128)} %param.13) | copy-start | bytes 1156
  11.2 1.7 %copy-start.8 = (s32[2,8]{1,0:T(2,128)S(1)}, s32[2,8]{1,0:T(2,128)}, u32[]{:S(2)}) copy-start(s32[2,8]{1,0:T(2,128)} %param.14) | copy-start | bytes 196
  11.2 1.9 %copy-start = (f32[144,144]{1,0:T(8,128)S(1)}, f32[144,144]{1,0:T(8,128)}, u32[]{:S(2)}) copy-start(f32[144,144]{1,0:T(8,128)} %constant.7.clone.sel_ref) | copy-start | bytes 248836
  11.2 1.8 %copy-start.1 = (f32[144,144]{1,0:T(8,128)S(1)}, f32[144,144]{1,0:T(8,128)}, u32[]{:S(2)}) copy-start(f32[144,144]{1,0:T(8,128)} %constant.8.clone.selt_ref) | copy-start | bytes 248836
  11.2 1.8 %copy-start.2 = (s32[4]{0:T(128)S(1)}, s32[4]{0:T(128)}, u32[]{:S(2)}) copy-start(s32[4]{0:T(128)} %dil_ref.1) | copy-start | bytes 52
where the time goes:
time: 126 us; the launch traced here: 125 us
  Pallas kernels  111 us (88%)
  local copies, waits for them, and re-layouts  13.3 us (11%)
    pallas_call x1, Pallas kernels, on_device(): pl.pallas_call(functools.partial(kernel, (nrow, ncol, rows, total_cells,...  111 us
    unnamed x35, local copies, waits for them, and re-layouts  7.35 us

commit v1 on v0

v1 whole, which is shorter than its diff:
```python
import functools

import jax
import jax.numpy as jnp
import numpy as np
from jax import lax
from jax.experimental import pallas as pl
from jax.experimental.pallas import tpu as pltpu
from jax.sharding import PartitionSpec as P

DMAX = 8
LAYERS = 4
ITERS = 2
LANES = 128

step_rate = 0.25
norm_eps = 1e-06

MESH = pl.DeviceIdType.MESH
F32 = jnp.float32
BF16 = jnp.bfloat16
OTHERS = [0, 1, 2, 3, 5, 6, 7, 8]
PER_ITER = 2 * LAYERS + 2


def tap_list():
    return [(row_step, col_step) for row_step in (-1, 0, 1) for col_step in (-1, 0, 1)]


def split2(value):
    high = value.astype(BF16)
    return high, (value - high.astype(F32)).astype(BF16)


def kernel(
    cfg,
    dil_ref, design_ref, active_ref, film_ref, target_ref, lanes_ref, wt_ref, blk_ref, sel_ref, selt_ref,
    new_ref, obj_ref,
    edge_t, edge_b, halo_t, halo_b, edge_l, edge_r, halo_l, halo_r,
    side_l, side_r, state_s, xo, xt, xb, wbig, wside, wt_s, pre_s, adj_s, ee_s, bfw, bbk, h_s, hd_s,
    amp9, part, got, grad9, q_s, grad_t, ar1, ar1_src, ar2, ar2_src,
    send_sem, recv_sem, ar_send, ar_recv,
):
    nrow, ncol, rows, total_cells, total_entries = cfg
    nx = rows * 16
    my_r = lax.axis_index("rows")
    my_c = lax.axis_index("cols")

    def exists(m):
        dr, dc = m // 3 - 1, m % 3 - 1
        r, c = my_r + dr, my_c + dc
        return (r >= 0) & (r < nrow) & (c >= 0) & (c < ncol)

    def ident(m):
        dr, dc = m // 3 - 1, m % 3 - 1
        return (my_r + dr, my_c + dc)

    def desc(phase, m, src, dst):
        return pltpu.make_async_remote_copy(
            src_ref=src(m), dst_ref=dst(m),
            send_sem=send_sem.at[phase, m], recv_sem=recv_sem.at[phase, m],
            device_id=ident(m), device_id_type=MESH,
        )

    def start(phase, src, dst):
        for m in OTHERS:
            @pl.when(exists(m))
            def _():
                desc(phase, m, src, dst).start()

    def arrive(phase, src, dst):
        for m in OTHERS:
            @pl.when(exists(8 - m))
            def _():
                desc(phase, m, src, dst).wait_recv()

    def sent(phase, src, dst):
        for m in OTHERS:
            @pl.when(exists(m))
            def _():
                desc(phase, m, src, dst).wait_send()

    def state_refs(slot):
        el, er, hl, hr = edge_l.at[slot], edge_r.at[slot], halo_l.at[slot], halo_r.at[slot]
        D, R = DMAX, rows

        def src(m):
            return {
                0: lambda: el.at[pl.ds(0, D)], 1: lambda: edge_t.at[slot], 2: lambda: er.at[pl.ds(0, D)],
                3: lambda: el, 5: lambda: er,
                6: lambda: el.at[pl.ds(R - D, D)], 7: lambda: edge_b.at[slot], 8: lambda: er.at[pl.ds(R - D, D)],
            }[m]()

        def dst(m):
            return {
                0: lambda: hr.at[pl.ds(R + D, D)], 1: lambda: halo_b.at[slot], 2: lambda: hl.at[pl.ds(R + D, D)],
                3: lambda: hr.at[pl.ds(D, R)], 5: lambda: hl.at[pl.ds(D, R)],
                6: lambda: hr.at[pl.ds(0, D)], 7: lambda: halo_t.at[slot], 8: lambda: hl.at[pl.ds(0, D)],
            }[m]()

        return src, dst

    def amp_refs(_):
        return (lambda m: amp9.at[4]), (lambda m: amp9.at[8 - m])

    def part_refs(it):
        return (lambda m: part.at[it, m]), (lambda m: got.at[it, 8 - m])

    def grad_refs(it):
        return (lambda m: grad_t.at[it]), (lambda m: grad9.at[it, 8 - m])

    nslot = ITERS * 2 * LAYERS
    zt = jnp.zeros((DMAX, 16, LANES), BF16)
    zh = jnp.zeros((rows + 2 * DMAX, LANES), F32)

    def clear(slot, _):
        halo_t[slot] = zt
        halo_b[slot] = zt
        halo_l[slot] = zh
        halo_r[slot] = zh
        return 0

    lax.fori_loop(0, nslot, clear, 0)
    z9 = jnp.zeros((9, 16, LANES), F32)
    amp9[...] = z9
    for it in range(ITERS):
        got[it] = z9
        grad9[it] = z9

    barrier = pltpu.get_barrier_semaphore()

    def greet(r, c):
        pl.semaphore_signal(barrier, inc=1, device_id=(r, c), device_id_type=MESH)

    for k in range(1, ncol):
        greet(my_r, lax.rem(my_c + k, ncol))
    for k in range(1, nrow):
        greet(lax.rem(my_r + k, nrow), my_c)
    greeted = (ncol - 1) + (nrow - 1)
    for m in (0, 2, 6, 8):
        there = exists(m)
        greeted = greeted + jnp.where(there, 1, 0)

        @pl.when(there)
        def _():
            greet(*ident(m))

    x_zero = jnp.zeros((DMAX, 16, 384), BF16)
    xo[0:DMAX] = x_zero
    xo[rows + DMAX : rows + 2 * DMAX] = x_zero
    xt[DMAX : 2 * DMAX] = x_zero
    xb[0:DMAX] = x_zero
    spread_ch = (
        lax.broadcasted_iota(jnp.int32, (16, LANES), 1) % 16 == lax.broadcasted_iota(jnp.int32, (16, LANES), 0)
    ).astype(F32).astype(BF16)
    wt_s[...] = jnp.dot(wt_ref[...], spread_ch, preferred_element_type=F32).reshape(2, LAYERS, 9, 16, LANES)
    pos = lax.broadcasted_iota(jnp.int32, (LANES, 16 * LANES), 0)
    col = lax.broadcasted_iota(jnp.int32, (LANES, 16 * LANES), 1)
    ee_s[...] = (pos == (col // LANES) * 8 + (col % LANES) // 16).astype(F32).astype(BF16)
    for t in range(9):
        b = blk_ref[t]
        bh, bl = split2(b)
        bh, bl = bh.astype(F32), bl.astype(F32)
        bfw[t] = jnp.concatenate([bh, bh, bl], axis=0).astype(BF16)
        bbk[t] = jnp.concatenate([bh, bl, bh], axis=1).astype(BF16)

    amp9[4] = design_ref[...] * active_ref[...]
    new_ref[...] = design_ref[...]
    pl.semaphore_wait(barrier, greeted)
    amp_phase = ITERS * PER_ITER
    start(amp_phase, *amp_refs(0))

    lane = lax.broadcasted_iota(jnp.int32, (24, 16, LANES), 2) // 16
    jpos = lax.broadcasted_iota(jnp.int32, (24, 16, LANES), 0) - 8 - lane
    for l in range(LAYERS):
        d = dil_ref[l]
        masks = [jpos == rx * d for rx in (-1, 0, 1)]
        for f in range(2):
            for ry in range(3):
                acc = jnp.zeros((24, 16, LANES), F32)
                for rx in range(3):
                    acc = jnp.where(masks[rx], wt_s[f, l, 3 * ry + rx][None], acc)
                banded = acc.astype(BF16).reshape(384, LANES)
                wbig[f, l, ry] = banded
                wside[f, l, 0, 128 * ry : 128 * ry + 128] = banded[0:128]
                wside[f, l, 1, 128 * ry : 128 * ry + 128] = banded[256:384]
    ones_block = (
        lax.broadcasted_iota(jnp.int32, (LANES, LANES), 0) // 16
        == lax.broadcasted_iota(jnp.int32, (LANES, LANES), 1) // 16
    ).astype(F32).astype(BF16)

    lw = lanes_ref[0:1, :]
    lb = lanes_ref[1:2, :]
    ro = lanes_ref[2:3, :]

    def shifted(value):
        c0, c1 = value[:, 0:8], value[:, 8:16]
        bs = lax.broadcasted_iota(jnp.int32, c0.shape, 1)
        l0 = jnp.where(bs == 0, 0.0, pltpu.roll(c1, 1, 1))
        r1 = jnp.where(bs == 7, 0.0, pltpu.roll(c0, 7, 1))
        return (
            jnp.concatenate([l0, c0], axis=1).astype(BF16),
            value.astype(BF16),
            jnp.concatenate([c1, r1], axis=1).astype(BF16),
        )

    def conv(slot, phase, f, l, value):
        refs = state_refs(slot)
        v3 = value.reshape(rows, 16, LANES)
        state_s[...] = v3
        edge_t[slot] = v3[0:DMAX].astype(BF16)
        edge_b[slot] = v3[rows - DMAX : rows].astype(BF16)
        edge_l[slot] = state_s[:, 0, :]
        edge_r[slot] = state_s[:, 15, :]
        start(phase, *refs)
        for n, piece in enumerate(shifted(v3)):
            xo[DMAX : rows + DMAX, :, 128 * n : 128 * n + 128] = piece
        d = dil_ref[l]
        out = None
        for ry in range(3):
            lhs = xo[pl.ds(DMAX + (ry - 1) * d, rows)].reshape(nx, 384)
            term = jnp.dot(lhs, wbig[f, l, ry], preferred_element_type=F32)
            out = term if out is None else out + term
        out = out.reshape(rows, 16, LANES)
        arrive(phase, *refs)
        for n, piece in enumerate(shifted(halo_t[slot].astype(F32))):
            xt[0:DMAX, :, 128 * n : 128 * n + 128] = piece
        for n, piece in enumerate(shifted(halo_b[slot].astype(F32))):
            xb[DMAX : 2 * DMAX, :, 128 * n : 128 * n + 128] = piece
        sides = []
        for n, (halo, side) in enumerate(((halo_l, side_l), (halo_r, side_r))):
            side[...] = halo[slot]
            lhs = jnp.concatenate(
                [side[pl.ds(DMAX + (ry - 1) * d, rows), :] for ry in range(3)], axis=1
            ).astype(BF16)
            sides.append(jnp.dot(lhs, wside[f, l, n], preferred_element_type=F32))
        top = jnp.dot(xt[pl.ds(DMAX - d, DMAX)].reshape(16 * DMAX, 384), wbig[f, l, 0], preferred_element_type=F32)
        bot = jnp.dot(xb[pl.ds(d, DMAX)].reshape(16 * DMAX, 384), wbig[f, l, 2], preferred_element_type=F32)
        out = jnp.concatenate(
            [
                out[0:DMAX] + top.reshape(DMAX, 16, LANES),
                out[DMAX : rows - DMAX],
                out[rows - DMAX : rows] + bot.reshape(DMAX, 16, LANES),
            ],
            axis=0,
        )
        bs = lax.broadcasted_iota(jnp.int32, (rows, 8, LANES), 1)
        add0 = jnp.where(bs == 0, sides[0][:, None, :], 0.0)
        add1 = jnp.where(bs == 7, sides[1][:, None, :], 0.0)
        return (out + jnp.concatenate([add0, add1], axis=1)).reshape(nx, LANES)

    def sigmoid(v):
        return 1.0 / (1.0 + jnp.exp(-v))

    def render(amp, dest):
        high, low = split2(amp.reshape(144, LANES))
        high, low = high.astype(F32), low.astype(F32)
        packed = (high + pltpu.roll(low, 16, 1) + pltpu.roll(high, 32, 1)).astype(BF16)
        picked = jnp.dot(sel_ref[...], packed, preferred_element_type=F32).astype(BF16)
        height = None
        for t in range(9):
            term = jnp.dot(picked[16 * t : 16 * t + 16, 0:48], bfw[t], preferred_element_type=F32)
            height = term if height is None else height + term
        two = jnp.concatenate([height[:, 0:128], height[:, 128:256]], axis=0)
        high, low = split2(two)
        spread = jnp.dot(high, ee_s[...], preferred_element_type=F32)
        spread = spread + jnp.dot(low, ee_s[...], preferred_element_type=F32)
        for s in range(2):
            for k in range(16):
                q = 16 * s + k
                y, xh = q // 2, q % 2
                for a in range(rows // 16):
                    dest[16 * a + y, 8 * xh : 8 * xh + 8, :] = spread[
                        16 * s + 8 * a : 16 * s + 8 * a + 8, 128 * k : 128 * k + 128
                    ]

    arrive(amp_phase, *amp_refs(0))
    render(amp9[...], h_s)
    sent(amp_phase, *amp_refs(0))

    def step(it, _):
        base = it * PER_ITER
        slot0 = it * 2 * LAYERS
        h = h_s[...].reshape(nx, LANES)
        state = (lw * h + lb + film_ref[...].astype(F32).reshape(nx, LANES)).astype(BF16).astype(F32)
        for l in range(LAYERS):
            pre = conv(slot0 + l, base + l, 0, l, state) + lanes_ref[4 + l : 5 + l, :]
            pre_s[l] = pre
            state = (state + pre * sigmoid(pre)).astype(BF16).astype(F32)
        pressure = None
        for piece in split2(ro * state):
            term = jnp.dot(piece, ones_block, preferred_element_type=F32)
            pressure = term if pressure is None else pressure + term
        misfit = pressure - target_ref[...].reshape(nx, LANES)
        miss = jnp.sum(misfit * misfit, keepdims=True) * (0.5 / 16)
        adjoint = ro * (misfit * (1.0 / 256.0))
        for n in range(LAYERS):
            l = LAYERS - 1 - n
            v = pre_s[l]
            s = sigmoid(v)
            slope = (adjoint * (s * (1.0 + v * (1.0 - s)))).astype(BF16).astype(F32)
            adjoint = adjoint + conv(slot0 + LAYERS + n, base + LAYERS + n, 1, l, slope)
        adj_s[...] = (lw * adjoint).reshape(rows, 16, LANES)
        strips = []
        for s in range(2):
            tiles = []
            for k in range(16):
                q = 16 * s + k
                y, xh = q // 2, q % 2
                tiles.append(
                    jnp.concatenate(
                        [adj_s[16 * a + y, 8 * xh : 8 * xh + 8, :] for a in range(rows // 16)], axis=0
                    )
                )
            strips.append(jnp.concatenate(tiles, axis=1))
        both = jnp.concatenate(strips, axis=0)
        folded = None
        for piece in split2(both):
            term = lax.dot_general(piece, ee_s[...], (((1,), (1,)), ((), ())), preferred_element_type=F32)
            folded = term if folded is None else folded + term
        hg = jnp.concatenate([folded[0:16], folded[16:32]], axis=1)
        high, low = split2(hg)
        wide = jnp.concatenate([high, high, low], axis=1)
        q_s[...] = jnp.zeros((144, LANES), F32)
        for t in range(9):
            q_s[16 * t : 16 * t + 16, 0:16] = lax.dot_general(
                wide, bbk[t], (((1,), (1,)), ((), ())), preferred_element_type=F32
            )
        mine = None
        for piece in split2(q_s[...]):
            term = jnp.dot(selt_ref[...], piece, preferred_element_type=F32)
            mine = term if mine is None else mine + term
        mine = mine.reshape(9, 16, LANES)
        part[it] = mine
        p_phase = base + 2 * LAYERS
        start(p_phase, *part_refs(it))
        got[it, 4] = mine[4]
        arrive(p_phase, *part_refs(it))
        gradient = jnp.sum(got[it], axis=0) * active_ref[...]
        squares = jnp.sum(gradient * gradient, keepdims=True)
        sub = lax.broadcasted_iota(jnp.int32, (8, LANES), 0)
        tile = jnp.where(sub == 0, squares, miss)
        ar1_src[it] = tile
        g_phase = p_phase + 1

        def ring(n, src, dst, dev):
            return pltpu.make_async_remote_copy(
                src_ref=src.at[it], dst_ref=dst,
                send_sem=ar_send.at[it, n], recv_sem=ar_recv.at[it, n],
                device_id=dev, device_id_type=MESH,
            )

        for k in range(1, ncol):
            ring(0, ar1_src, ar1.at[it, my_c], (my_r, lax.rem(my_c + k, ncol))).start()
        ar1[it, my_c] = tile
        more = it < ITERS - 1

        @pl.when(more)
        def _():
            grad_t[it] = gradient
            start(g_phase, *grad_refs(it))
            grad9[it, 4] = gradient

        many = ar1.at[it, pl.ds(0, ncol - 1)]
        pltpu.make_async_copy(many, many, ar_recv.at[it, 0]).wait()
        tile2 = jnp.sum(ar1[it], axis=0)
        ar2_src[it] = tile2
        for k in range(1, nrow):
            ring(1, ar2_src, ar2.at[it, my_r], (lax.rem(my_r + k, nrow), my_c)).start()
        ar2[it, my_r] = tile2

        @pl.when(more)
        def _():
            arrive(g_phase, *grad_refs(it))
            render(grad9[it], hd_s)

        many = ar2.at[it, pl.ds(0, nrow - 1)]
        pltpu.make_async_copy(many, many, ar_recv.at[it, 1]).wait()
        total = jnp.sum(ar2[it], axis=0)
        scale = step_rate / jnp.sqrt(total[0:1] * (1.0 / total_entries) + norm_eps)
        obj_ref[it] = total * (1.0 / total_cells)
        new_ref[...] = new_ref[...] - gradient * scale

        @pl.when(more)
        def _():
            h_s[...] = h_s[...] - hd_s[...] * scale[None]

        return 0

    lax.fori_loop(0, ITERS, step, 0)

    def drain(it, _):
        base = it * PER_ITER
        for n in range(2 * LAYERS):
            sent(base + n, *state_refs(it * 2 * LAYERS + n))
        sent(base + 2 * LAYERS, *part_refs(it))

        @pl.when(it < ITERS - 1)
        def _():
            sent(base + 2 * LAYERS + 1, *grad_refs(it))

        many = ar1.at[it, pl.ds(0, ncol - 1)]
        pltpu.make_async_copy(many, many, ar_send.at[it, 0]).wait()
        many = ar2.at[it, pl.ds(0, nrow - 1)]
        pltpu.make_async_copy(many, many, ar_send.at[it, 1]).wait()
        return 0

    lax.fori_loop(0, ITERS, drain, 0)


def select_matrix(dr_count, dc_count):
    sel = np.zeros((9, dr_count, dc_count, 9, dr_count, dc_count), np.float32)
    for t, (ry, rx) in enumerate(tap_list()):
        for a in range(dr_count):
            for b in range(dc_count):
                ta, tb = a + ry, b + rx
                nr, nc = ta // dr_count, tb // dc_count
                sel[t, a, b, 3 * (nr + 1) + nc + 1, ta - nr * dr_count, tb - nc * dc_count] = 1
    size = 9 * dr_count * dc_count
    return sel.reshape(size, size)


def basis_blocks(stamp_basis):
    nparams, side = stamp_basis.shape[0], stamp_basis.shape[1] // 2
    half = side // 2
    padded = jnp.pad(stamp_basis, ((0, 16 - nparams), (half, half), (half, half)))
    windows = padded.reshape(16, 3, side, 3, side).transpose(1, 3, 0, 2, 4)
    return windows[::-1, ::-1].reshape(9, 16, side * side)


def on_device(
    design, active, stamp_basis, film_field, lift_weight, lift_bias, conv_weight, conv_bias, readout, target, dilation
):
    channels, rows, cols = film_field.shape
    nparams, drows, dcols = design.shape
    nrow = lax.axis_size("rows")
    ncol = lax.axis_size("cols")
    ndev = nrow * ncol
    total_cells = rows * cols * ndev
    total_entries = nparams * drows * dcols * ndev

    def by_dimple(v):
        v = v.reshape(nparams, drows * dcols).T
        return jnp.pad(v, ((0, 0), (0, LANES - nparams)))

    design_t = by_dimple(design)
    active_t = jnp.broadcast_to(active.astype(F32).reshape(drows * dcols, 1), (drows * dcols, LANES))
    film = film_field.reshape(channels, rows, dcols, 2, 8).transpose(1, 3, 2, 4, 0).reshape(rows, 16, LANES)
    targ = target.reshape(rows, dcols, 2, 8).transpose(0, 2, 1, 3).reshape(rows, 16, 8, 1)
    targ = jnp.broadcast_to(targ, (rows, 16, 8, 16)).reshape(rows, 16, LANES)
    lanes = jnp.concatenate(
        [jnp.tile(jnp.stack([lift_weight, lift_bias, readout, readout]), (1, 8)), jnp.tile(conv_bias, (1, 8))]
    )
    wt = jnp.stack([jnp.swapaxes(conv_weight, 2, 3), conv_weight[:, ::-1]])
    wt = wt.reshape(2 * LAYERS * 9 * channels, channels)
    blocks = basis_blocks(stamp_basis)
    sel = select_matrix(drows, dcols).astype(BF16)

    nslot = ITERS * 2 * LAYERS
    phases = ITERS * PER_ITER + 1
    tall = rows + 2 * DMAX
    vmem = pl.BlockSpec(memory_space=pltpu.VMEM)
    new, obj = pl.pallas_call(
        functools.partial(kernel, (nrow, ncol, rows, total_cells, total_entries)),
        out_shape=(
            jax.ShapeDtypeStruct((16, LANES), F32),
            jax.ShapeDtypeStruct((ITERS, 8, LANES), F32),
        ),
        in_specs=[pl.BlockSpec(memory_space=pltpu.SMEM)] + [vmem] * 9,
        out_specs=(vmem, vmem),
        scratch_shapes=[
            pltpu.VMEM((nslot, DMAX, 16, LANES), BF16),
            pltpu.VMEM((nslot, DMAX, 16, LANES), BF16),
            pltpu.VMEM((nslot, DMAX, 16, LANES), BF16),
            pltpu.VMEM((nslot, DMAX, 16, LANES), BF16),
            pltpu.VMEM((nslot, rows, LANES), F32),
            pltpu.VMEM((nslot, rows, LANES), F32),
            pltpu.VMEM((nslot, tall, LANES), F32),
            pltpu.VMEM((nslot, tall, LANES), F32),
            pltpu.VMEM((tall, LANES), F32),
            pltpu.VMEM((tall, LANES), F32),
            pltpu.VMEM((rows, 16, LANES), F32),
            pltpu.VMEM((tall, 16, 384), BF16),
            pltpu.VMEM((2 * DMAX, 16, 384), BF16),
            pltpu.VMEM((2 * DMAX, 16, 384), BF16),
            pltpu.VMEM((2, LAYERS, 3, 384, LANES), BF16),
            pltpu.VMEM((2, LAYERS, 2, 384, LANES), BF16),
            pltpu.VMEM((2, LAYERS, 9, 16, LANES), F32),
            pltpu.VMEM((LAYERS, rows * 16, LANES), F32),
            pltpu.VMEM((rows, 16, LANES), F32),
            pltpu.VMEM((LANES, 16 * LANES), BF16),
            pltpu.VMEM((9, 48, 256), BF16),
            pltpu.VMEM((9, 16, 768), BF16),
            pltpu.VMEM((rows, 16, LANES), F32),
            pltpu.VMEM((rows, 16, LANES), F32),
            pltpu.VMEM((9, 16, LANES), F32),
            pltpu.VMEM((ITERS, 9, 16, LANES), F32),
            pltpu.VMEM((ITERS, 9, 16, LANES), F32),
            pltpu.VMEM((ITERS, 9, 16, LANES), F32),
            pltpu.VMEM((144, LANES), F32),
            pltpu.VMEM((ITERS, 16, LANES), F32),
            pltpu.VMEM((ITERS, ncol, 8, LANES), F32),
            pltpu.VMEM((ITERS, 8, LANES), F32),
            pltpu.VMEM((ITERS, nrow, 8, LANES), F32),
            pltpu.VMEM((ITERS, 8, LANES), F32),
            pltpu.SemaphoreType.DMA((phases, 9)),
            pltpu.SemaphoreType.DMA((phases, 9)),
            pltpu.SemaphoreType.DMA((ITERS, 2)),
            pltpu.SemaphoreType.DMA((ITERS, 2)),
        ],
        compiler_params=pltpu.CompilerParams(
            collective_id=0, has_side_effects=True, vmem_limit_bytes=40 * 1024 * 1024
        ),
    )(dilation, design_t, active_t, film, targ, lanes, wt, blocks, sel, sel.T)
    new_design = new[:, :nparams].T.reshape(nparams, drows, dcols)
    return new_design, obj[:, 1, 0]


def solution(mesh):
    placed = (
        P(None, "rows", "cols"),
        P("rows", "cols"),
        P(),
        P(None, "rows", "cols"),
        P(),
        P(),
        P(),
        P(),
        P(),
        P("rows", "cols"),
        P(),
    )
    return jax.shard_map(
        on_device,
        mesh=mesh,
        in_specs=placed,
        out_specs=(P(None, "rows", "cols"), P()),
        check_vma=False,
    )
```

time: 126 us -> 113 us (0.90)
  Pallas kernels: 111 us -> 104 us
  local copies, waits for them, and re-layouts: 13.3 us -> 7.84 us
    pallas_call x1, Pallas kernels: 111 us -> 104 us  [on_device(): pl.pallas_call(functools.partial(kernel, (nrow, ncol, rows, total_cells,...]
    unnamed x35 -> x27, local copies, waits for them, and re-layouts: 7.35 us -> 1.09 us
    another operation x3 -> x0, local copies, waits for them, and re-layouts: 2.99 us -> none  [the longest x2 2.17 us: on_device(): wt = jnp.tile(wt, (1, 1, 1, 1, 8))]
    rev x0 -> x2, local copies, waits for them, and re-layouts: none -> 2.01 us  [basis_blocks(): return windows[::-1, ::-1].reshape(9, 16, side * side)]
where the time goes in v1:
time: 113 us
  Pallas kernels  104 us (92%)
  local copies, waits for them, and re-layouts  7.84 us (7%)
    pallas_call x1, Pallas kernels, on_device(): pl.pallas_call(functools.partial(kernel, (nrow, ncol, rows, total_cells,...  104 us

profile of v1, /device:TPU:0, one launch (start us, length us, event | category | flops | bytes accessed | tf_op | source)
XLA Modules:
  0.0 112.7 jit_solution(7131211215592517929)
XLA Ops:
  0.6 1.0 pad.9
  1.6 0.6 reshape.49
  2.2 1.9 %rev.7 = f32[3,3,16,16,16]{4,1,3,0,2:T(4,128)S(1)} reverse(f32[3,3,16,16,16]{4,1,3,0,2:T(4,128)S(1)} %bitcast.29), dimensions={0,1} | reverse | bytes 294912 | tf_op jit(solution)/shard_map/rev | solution.py:428
  4.1 0.0 copy-start.5
  4.1 0.1 copy.26
  4.2 0.5 reshape.50.blk_ref
  4.7 0.1 copy-done.5
  4.8 0.1 copy.23
  4.9 0.1 broadcast_in_dim.17
  5.0 0.0 copy-start.3
  5.0 0.3 copy.28.target_ref
  5.4 0.4 copy-done.4
  5.7 0.3 copy.21
  6.1 0.0 copy-start.9
  6.1 0.0 copy-start.10
  6.1 0.0 copy-start.7
  6.1 0.0 copy-start.6
  6.1 0.0 copy-start
  6.1 0.0 copy-start.1
  6.2 0.0 copy-start.2
  6.2 0.3 copy.22
  6.5 0.2 copy.27.film_ref
  6.8 0.1 copy.25
  6.9 0.1 pad_maximum_fusion
  7.1 0.1 tile.9
  7.1 0.1 tile.21
  7.2 0.1 copy.30
  7.3 0.1 broadcast_in_dim.14
  7.4 0.1 broadcast_in_dim.15.active_ref
  7.5 103.9 %shard_map.140 = (f32[16,128]{1,0:T(8,128)S(1)}, f32[2,8,128]{2,1,0:T(8,128)S(1)}) custom-call(s32[4]{0:T(128)S(1)} %copy-done.2, f32[16,128]{1,0:T(8,128)S(1)} %pad.8.design_ref, f32[16,128]{1,0:T(8,128)S(1)} %broadcast_in_dim.15.active_ref, bf16[32,16,128]{2,1,0:T(8,128)(2,1)S(1)} %copy.27.film_ref, f32[32,16,128]{2,1,0:T(8,128)S(1)} %copy.28.target_ref, ...), custom_call_target="tpu_custom_call" | custom-call | tf_op jit(solution)/shard_map/pallas_call | solution.py:463
  111.4 0.7 copy.31
  112.1 0.6 slice_reduce_fusion
  (22 shorter events, 0.1 us)
Async XLA Ops:
  4.1 0.7 copy-start.5
  4.8 0.9 copy-start.4
  5.0 1.7 %copy-start.3 = (bf16[4,9,16,16]{3,2,1,0:T(8,128)(2,1)S(1)}, bf16[4,9,16,16]{3,2,1,0:T(8,128)(2,1)}, u32[]{:S(2)}) copy-start(bf16[4,9,16,16]{3,2,1,0:T(8,128)(2,1)} %param.19) | copy-start | bytes 55300
  6.1 0.9 copy-start.9
  6.1 0.9 copy-start.10
  6.1 0.9 copy-start.11
  6.1 1.0 copy-start.7
  6.1 1.1 %copy-start.6 = (f32[6,2,8]{2,1,0:T(2,128)S(1)}, f32[6,2,8]{2,1,0:T(2,128)}, u32[]{:S(2)}) copy-start(f32[6,2,8]{2,1,0:T(2,128)} %param.13) | copy-start | bytes 1156
  6.1 1.2 %copy-start.8 = (s32[2,8]{1,0:T(2,128)S(1)}, s32[2,8]{1,0:T(2,128)}, u32[]{:S(2)}) copy-start(s32[2,8]{1,0:T(2,128)} %param.14) | copy-start | bytes 196
  6.1 1.4 %copy-start = (bf16[144,144]{1,0:T(8,128)(2,1)S(1)}, bf16[144,144]{1,0:T(8,128)(2,1)}, u32[]{:S(2)}) copy-start(bf16[144,144]{1,0:T(8,128)(2,1)} %constant.7.clone.sel_ref) | copy-start | bytes 124420
  6.1 1.4 %copy-start.1 = (bf16[144,144]{1,0:T(8,128)(2,1)S(1)}, bf16[144,144]{1,0:T(8,128)(2,1)}, u32[]{:S(2)}) copy-start(bf16[144,144]{1,0:T(8,128)(2,1)} %constant.8.clone.selt_ref) | copy-start | bytes 124420
  6.2 1.4 %copy-start.2 = (s32[4]{0:T(128)S(1)}, s32[4]{0:T(128)}, u32[]{:S(2)}) copy-start(s32[4]{0:T(128)} %dil_ref.1) | copy-start | bytes 52

commit v2 on v1

--- a/solution.py
+++ b/solution.py
@@ -20,7 +20,9 @@
 F32 = jnp.float32
 BF16 = jnp.bfloat16
 OTHERS = [0, 1, 2, 3, 5, 6, 7, 8]
-PER_ITER = 2 * LAYERS + 2
+PAIRS = LAYERS // 2
+PER_ITER = 2 * PAIRS + 2
+HALO = 2 * DMAX
 
 
 def tap_list():
@@ -37,7 +39,7 @@
     dil_ref, design_ref, active_ref, film_ref, target_ref, lanes_ref, wt_ref, blk_ref, sel_ref, selt_ref,
     new_ref, obj_ref,
     edge_t, edge_b, halo_t, halo_b, edge_l, edge_r, halo_l, halo_r,
-    side_l, side_r, state_s, xo, xt, xb, wbig, wside, wt_s, pre_s, adj_s, ee_s, bfw, bbk, h_s, hd_s,
+    cf_s, side_s, xo, xn, wbig, wside, wt_s, pre_o, pre_c, pre_w, adj_s, ee_s, bfw, bbk, h_s, hd_s,
     amp9, part, got, grad9, q_s, grad_t, ar1, ar1_src, ar2, ar2_src,
     send_sem, recv_sem, ar_send, ar_recv,
 ):
@@ -80,22 +82,27 @@
             def _():
                 desc(phase, m, src, dst).wait_send()
 
-    def state_refs(slot):
-        el, er, hl, hr = edge_l.at[slot], edge_r.at[slot], halo_l.at[slot], halo_r.at[slot]
-        D, R = DMAX, rows
+    def state_refs(slot, both):
+        n, g = (HALO + DMAX, 3) if both else (HALO, 2)
+        H, R = HALO, rows
+        el, er, hl, hr = [ref.at[slot, pl.ds(0, g)] for ref in (edge_l, edge_r, halo_l, halo_r)]
+        et, eb, ht, hb = [ref.at[slot, pl.ds(0, n)] for ref in (edge_t, edge_b, halo_t, halo_b)]
+
+        def cut(ref, at, size):
+            return ref.at[:, pl.ds(at, size)]
 
         def src(m):
             return {
-                0: lambda: el.at[pl.ds(0, D)], 1: lambda: edge_t.at[slot], 2: lambda: er.at[pl.ds(0, D)],
+                0: lambda: cut(el, 0, H), 1: lambda: et, 2: lambda: cut(er, 0, H),
                 3: lambda: el, 5: lambda: er,
-                6: lambda: el.at[pl.ds(R - D, D)], 7: lambda: edge_b.at[slot], 8: lambda: er.at[pl.ds(R - D, D)],
+                6: lambda: cut(el, R - H, H), 7: lambda: eb, 8: lambda: cut(er, R - H, H),
             }[m]()
 
         def dst(m):
             return {
-                0: lambda: hr.at[pl.ds(R + D, D)], 1: lambda: halo_b.at[slot], 2: lambda: hl.at[pl.ds(R + D, D)],
-                3: lambda: hr.at[pl.ds(D, R)], 5: lambda: hl.at[pl.ds(D, R)],
-                6: lambda: hr.at[pl.ds(0, D)], 7: lambda: halo_t.at[slot], 8: lambda: hl.at[pl.ds(0, D)],
+                0: lambda: cut(hr, R + H, H), 1: lambda: hb, 2: lambda: cut(hl, R + H, H),
+                3: lambda: cut(hr, H, R), 5: lambda: cut(hl, H, R),
+                6: lambda: cut(hr, 0, H), 7: lambda: ht, 8: lambda: cut(hl, 0, H),
             }[m]()
 
         return src, dst
@@ -109,9 +116,9 @@
     def grad_refs(it):
         return (lambda m: grad_t.at[it]), (lambda m: grad9.at[it, 8 - m])
 
-    nslot = ITERS * 2 * LAYERS
-    zt = jnp.zeros((DMAX, 16, LANES), BF16)
-    zh = jnp.zeros((rows + 2 * DMAX, LANES), F32)
+    nslot = ITERS * 2 * PAIRS
+    zt = jnp.zeros((HALO + DMAX, 16, LANES), BF16)
+    zh = jnp.zeros((3, rows + 2 * HALO, LANES), BF16)
 
     def clear(slot, _):
         halo_t[slot] = zt
@@ -145,11 +152,6 @@
         def _():
             greet(*ident(m))
 
-    x_zero = jnp.zeros((DMAX, 16, 384), BF16)
-    xo[0:DMAX] = x_zero
-    xo[rows + DMAX : rows + 2 * DMAX] = x_zero
-    xt[DMAX : 2 * DMAX] = x_zero
-    xb[0:DMAX] = x_zero
     spread_ch = (
         lax.broadcasted_iota(jnp.int32, (16, LANES), 1) % 16 == lax.broadcasted_iota(jnp.int32, (16, LANES), 0)
     ).astype(F32).astype(BF16)
@@ -158,7 +160,7 @@
     col = lax.broadcasted_iota(jnp.int32, (LANES, 16 * LANES), 1)
     ee_s[...] = (pos == (col // LANES) * 8 + (col % LANES) // 16).astype(F32).astype(BF16)
     for t in range(9):
-        b = blk_ref[t]
+        b = blk_ref[8 - t]
         bh, bl = split2(b)
         bh, bl = bh.astype(F32), bl.astype(F32)
         bfw[t] = jnp.concatenate([bh, bh, bl], axis=0).astype(BF16)
@@ -193,61 +195,102 @@
     lb = lanes_ref[1:2, :]
     ro = lanes_ref[2:3, :]
 
-    def shifted(value):
+    def shifted(value, left=None, right=None):
         c0, c1 = value[:, 0:8], value[:, 8:16]
         bs = lax.broadcasted_iota(jnp.int32, c0.shape, 1)
-        l0 = jnp.where(bs == 0, 0.0, pltpu.roll(c1, 1, 1))
-        r1 = jnp.where(bs == 7, 0.0, pltpu.roll(c0, 7, 1))
+        l0 = jnp.where(bs == 0, 0.0 if left is None else left[:, None, :], pltpu.roll(c1, 1, 1))
+        r1 = jnp.where(bs == 7, 0.0 if right is None else right[:, None, :], pltpu.roll(c0, 7, 1))
         return (
             jnp.concatenate([l0, c0], axis=1).astype(BF16),
             value.astype(BF16),
             jnp.concatenate([c1, r1], axis=1).astype(BF16),
         )
 
-    def conv(slot, phase, f, l, value):
-        refs = state_refs(slot)
-        v3 = value.reshape(rows, 16, LANES)
-        state_s[...] = v3
-        edge_t[slot] = v3[0:DMAX].astype(BF16)
-        edge_b[slot] = v3[rows - DMAX : rows].astype(BF16)
-        edge_l[slot] = state_s[:, 0, :]
-        edge_r[slot] = state_s[:, 15, :]
-        start(phase, *refs)
-        for n, piece in enumerate(shifted(v3)):
-            xo[DMAX : rows + DMAX, :, 128 * n : 128 * n + 128] = piece
+    def put(ref, at, pieces):
+        for n, piece in enumerate(pieces):
+            ref[at : at + piece.shape[0], :, 128 * n : 128 * n + 128] = piece
+
+    def conv_rows(ref, f, l, at, count):
         d = dil_ref[l]
         out = None
         for ry in range(3):
-            lhs = xo[pl.ds(DMAX + (ry - 1) * d, rows)].reshape(nx, 384)
+            lhs = ref[pl.ds(at + (ry - 1) * d, count)].reshape(16 * count, 384)
             term = jnp.dot(lhs, wbig[f, l, ry], preferred_element_type=F32)
             out = term if out is None else out + term
-        out = out.reshape(rows, 16, LANES)
+        return out.reshape(count, 16, LANES)
+
+    def f32(value):
+        return value.astype(F32)
+
+    tall = rows + 2 * DMAX
+
+    def wide_conv(slot, phase, f, l, v3, extra=None):
+        H, D, R = HALO, DMAX, rows
+        refs = state_refs(slot, extra is not None)
+        cf_s[H : H + R] = v3
+        edge_t[slot, 0:H] = v3[0:H].astype(BF16)
+        edge_b[slot, 0:H] = v3[R - H : R].astype(BF16)
+        for n, (gl, gr) in enumerate(((0, 15), (8, 7))):
+            edge_l[slot, n] = cf_s[H : H + R, gl, :].astype(BF16)
+            edge_r[slot, n] = cf_s[H : H + R, gr, :].astype(BF16)
+        if extra is not None:
+            adj_s[...] = extra
+            edge_t[slot, H : H + D] = extra[0:D].astype(BF16)
+            edge_b[slot, H : H + D] = extra[R - D : R].astype(BF16)
+            edge_l[slot, 2] = adj_s[:, 0, :].astype(BF16)
+            edge_r[slot, 2] = adj_s[:, 15, :].astype(BF16)
+        start(phase, *refs)
+        put(xo, H, shifted(v3))
+        mid = conv_rows(xo, f, l, H + D, R - 2 * D)
         arrive(phase, *refs)
-        for n, piece in enumerate(shifted(halo_t[slot].astype(F32))):
-            xt[0:DMAX, :, 128 * n : 128 * n + 128] = piece
-        for n, piece in enumerate(shifted(halo_b[slot].astype(F32))):
-            xb[DMAX : 2 * DMAX, :, 128 * n : 128 * n + 128] = piece
-        sides = []
-        for n, (halo, side) in enumerate(((halo_l, side_l), (halo_r, side_r))):
-            side[...] = halo[slot]
+        above, below = f32(halo_t[slot, 0:H]), f32(halo_b[slot, 0:H])
+        cf_s[0:H] = above
+        cf_s[H + R : 2 * H + R] = below
+        put(xo, 0, shifted(above))
+        put(xo, H + R, shifted(below))
+        top = conv_rows(xo, f, l, H - D, 2 * D)
+        bot = conv_rows(xo, f, l, H + R - D, 2 * D)
+        side_s[0] = f32(halo_l[slot, 1])
+        side_s[1] = f32(halo_l[slot, 0])
+        side_s[2] = cf_s[:, 0, :]
+        side_s[3] = cf_s[:, 15, :]
+        side_s[4] = f32(halo_r[slot, 0])
+        side_s[5] = f32(halo_r[slot, 1])
+        d = dil_ref[l]
+        outer = None
+        near = ([], [])
+        for ry in range(3):
+            six = [side_s[n, pl.ds(H - D + (ry - 1) * d, tall), :] for n in range(6)]
+            for n in range(2):
+                near[n].append(six[3 * n + 1])
             lhs = jnp.concatenate(
-                [side[pl.ds(DMAX + (ry - 1) * d, rows), :] for ry in range(3)], axis=1
+                [jnp.concatenate(six[0:3], axis=1), jnp.concatenate(six[3:6], axis=1)], axis=0
             ).astype(BF16)
-            sides.append(jnp.dot(lhs, wside[f, l, n], preferred_element_type=F32))
-        top = jnp.dot(xt[pl.ds(DMAX - d, DMAX)].reshape(16 * DMAX, 384), wbig[f, l, 0], preferred_element_type=F32)
-        bot = jnp.dot(xb[pl.ds(d, DMAX)].reshape(16 * DMAX, 384), wbig[f, l, 2], preferred_element_type=F32)
-        out = jnp.concatenate(
-            [
-                out[0:DMAX] + top.reshape(DMAX, 16, LANES),
-                out[DMAX : rows - DMAX],
-                out[rows - DMAX : rows] + bot.reshape(DMAX, 16, LANES),
-            ],
-            axis=0,
+            term = jnp.dot(lhs, wbig[f, l, ry], preferred_element_type=F32)
+            outer = term if outer is None else outer + term
+        inner = [
+            jnp.dot(
+                jnp.concatenate(near[n], axis=1).astype(BF16), wside[f, l, n], preferred_element_type=F32
+            )
+            for n in range(2)
+        ]
+        bs = lax.broadcasted_iota(jnp.int32, (tall, 8, LANES), 1)
+        add0 = jnp.where(bs == 0, inner[0][:, None, :], 0.0)
+        add1 = jnp.where(bs == 7, inner[1][:, None, :], 0.0)
+        out = jnp.concatenate([top, mid, bot], axis=0) + jnp.concatenate([add0, add1], axis=1)
+        return out, outer[0:tall], outer[tall : 2 * tall]
+
+    inside = [jnp.where(exists(m), 1.0, 0.0).astype(F32) for m in (1, 7, 3, 5)]
+
+    def clip_map(value):
+        D, R = DMAX, rows
+        return jnp.concatenate(
+            [value[0:D] * inside[0], value[D : D + R], value[D + R : 2 * D + R] * inside[1]], axis=0
         )
-        bs = lax.broadcasted_iota(jnp.int32, (rows, 8, LANES), 1)
-        add0 = jnp.where(bs == 0, sides[0][:, None, :], 0.0)
-        add1 = jnp.where(bs == 7, sides[1][:, None, :], 0.0)
-        return (out + jnp.concatenate([add0, add1], axis=1)).reshape(nx, LANES)
+
+    def near_conv(f, l, c3, left, right):
+        put(xn, 0, shifted(clip_map(c3), clip_map(left) * inside[2], clip_map(right) * inside[3]))
+        return conv_rows(xn, f, l, DMAX, rows)
 
     def sigmoid(v):
         return 1.0 / (1.0 + jnp.exp(-v))
@@ -280,27 +323,54 @@
 
     def step(it, _):
         base = it * PER_ITER
-        slot0 = it * 2 * LAYERS
-        h = h_s[...].reshape(nx, LANES)
-        state = (lw * h + lb + film_ref[...].astype(F32).reshape(nx, LANES)).astype(BF16).astype(F32)
-        for l in range(LAYERS):
-            pre = conv(slot0 + l, base + l, 0, l, state) + lanes_ref[4 + l : 5 + l, :]
-            pre_s[l] = pre
-            state = (state + pre * sigmoid(pre)).astype(BF16).astype(F32)
+        slot0 = it * 2 * PAIRS
+        D, R = DMAX, rows
+        state = f32((lw * h_s[...] + lb + f32(film_ref[...])).astype(BF16))
+        for n in range(PAIRS):
+            la, lb_ = 2 * n, 2 * n + 1
+            bias = lanes_ref[4 + la : 5 + la, :]
+            outs = wide_conv(slot0 + n, base + n, 0, la, state)
+            olds = (cf_s[D : D + tall], side_s[1, D : D + tall], side_s[4, D : D + tall])
+            news = []
+            for k in range(3):
+                pre = outs[k] + bias
+                if k == 0:
+                    pre_c[n] = pre
+                else:
+                    pre_w[n, k - 1] = pre
+                news.append(f32((olds[k] + pre * sigmoid(pre)).astype(BF16)))
+            pre = near_conv(0, lb_, *news) + lanes_ref[4 + lb_ : 5 + lb_, :]
+            pre_o[n] = pre
+            state = f32((news[0][D : D + R] + pre * sigmoid(pre)).astype(BF16))
         pressure = None
-        for piece in split2(ro * state):
+        for piece in split2((ro * state).reshape(nx, LANES)):
             term = jnp.dot(piece, ones_block, preferred_element_type=F32)
             pressure = term if pressure is None else pressure + term
         misfit = pressure - target_ref[...].reshape(nx, LANES)
         miss = jnp.sum(misfit * misfit, keepdims=True) * (0.5 / 16)
-        adjoint = ro * (misfit * (1.0 / 256.0))
-        for n in range(LAYERS):
-            l = LAYERS - 1 - n
-            v = pre_s[l]
+        adjoint = (ro * (misfit * (1.0 / 256.0))).reshape(rows, 16, LANES)
+
+        def slope_of(grad, v):
             s = sigmoid(v)
-            slope = (adjoint * (s * (1.0 + v * (1.0 - s)))).astype(BF16).astype(F32)
-            adjoint = adjoint + conv(slot0 + LAYERS + n, base + LAYERS + n, 1, l, slope)
-        adj_s[...] = (lw * adjoint).reshape(rows, 16, LANES)
+            return f32((grad * (s * (1.0 + v * (1.0 - s)))).astype(BF16))
+
+        for n in range(PAIRS):
+            pair = PAIRS - 1 - n
+            slot = slot0 + PAIRS + n
+            slope = slope_of(adjoint, pre_o[pair])
+            outs = wide_conv(slot, base + PAIRS + n, 1, 2 * pair + 1, slope, adjoint)
+            grown = jnp.concatenate(
+                [f32(halo_t[slot, HALO : HALO + D]), adjoint, f32(halo_b[slot, HALO : HALO + D])], axis=0
+            )
+            adjs = (
+                grown + outs[0],
+                f32(halo_l[slot, 2])[D : D + tall] + outs[1],
+                f32(halo_r[slot, 2])[D : D + tall] + outs[2],
+            )
+            pres = (pre_c[pair], pre_w[pair, 0], pre_w[pair, 1])
+            slopes = [slope_of(x, v) for x, v in zip(adjs, pres)]
+            adjoint = adjs[0][D : D + R] + near_conv(1, 2 * pair, *slopes)
+        adj_s[...] = lw * adjoint
         strips = []
         for s in range(2):
             tiles = []
@@ -332,7 +402,7 @@
             mine = term if mine is None else mine + term
         mine = mine.reshape(9, 16, LANES)
         part[it] = mine
-        p_phase = base + 2 * LAYERS
+        p_phase = base + 2 * PAIRS
         start(p_phase, *part_refs(it))
         got[it, 4] = mine[4]
         arrive(p_phase, *part_refs(it))
@@ -391,13 +461,13 @@
 
     def drain(it, _):
         base = it * PER_ITER
-        for n in range(2 * LAYERS):
-            sent(base + n, *state_refs(it * 2 * LAYERS + n))
-        sent(base + 2 * LAYERS, *part_refs(it))
+        for n in range(2 * PAIRS):
+            sent(base + n, *state_refs(it * 2 * PAIRS + n, n >= PAIRS))
+        sent(base + 2 * PAIRS, *part_refs(it))
 
         @pl.when(it < ITERS - 1)
         def _():
-            sent(base + 2 * LAYERS + 1, *grad_refs(it))
+            sent(base + 2 * PAIRS + 1, *grad_refs(it))
 
         many = ar1.at[it, pl.ds(0, ncol - 1)]
         pltpu.make_async_copy(many, many, ar_send.at[it, 0]).wait()
@@ -425,7 +495,7 @@
     half = side // 2
     padded = jnp.pad(stamp_basis, ((0, 16 - nparams), (half, half), (half, half)))
     windows = padded.reshape(16, 3, side, 3, side).transpose(1, 3, 0, 2, 4)
-    return windows[::-1, ::-1].reshape(9, 16, side * side)
+    return windows.reshape(9, 16, side * side)
 
 
 def on_device(
@@ -456,7 +526,7 @@
     blocks = basis_blocks(stamp_basis)
     sel = select_matrix(drows, dcols).astype(BF16)
 
-    nslot = ITERS * 2 * LAYERS
+    nslot = ITERS * 2 * PAIRS
     phases = ITERS * PER_ITER + 1
     tall = rows + 2 * DMAX
     vmem = pl.BlockSpec(memory_space=pltpu.VMEM)
@@ -469,24 +539,24 @@
         in_specs=[pl.BlockSpec(memory_space=pltpu.SMEM)] + [vmem] * 9,
         out_specs=(vmem, vmem),
         scratch_shapes=[
-            pltpu.VMEM((nslot, DMAX, 16, LANES), BF16),
-            pltpu.VMEM((nslot, DMAX, 16, LANES), BF16),
-            pltpu.VMEM((nslot, DMAX, 16, LANES), BF16),
-            pltpu.VMEM((nslot, DMAX, 16, LANES), BF16),
-            pltpu.VMEM((nslot, rows, LANES), F32),
-            pltpu.VMEM((nslot, rows, LANES), F32),
-            pltpu.VMEM((nslot, tall, LANES), F32),
-            pltpu.VMEM((nslot, tall, LANES), F32),
-            pltpu.VMEM((tall, LANES), F32),
-            pltpu.VMEM((tall, LANES), F32),
-            pltpu.VMEM((rows, 16, LANES), F32),
+            pltpu.VMEM((nslot, HALO + DMAX, 16, LANES), BF16),
+            pltpu.VMEM((nslot, HALO + DMAX, 16, LANES), BF16),
+            pltpu.VMEM((nslot, HALO + DMAX, 16, LANES), BF16),
+            pltpu.VMEM((nslot, HALO + DMAX, 16, LANES), BF16),
+            pltpu.VMEM((nslot, 3, rows, LANES), BF16),
+            pltpu.VMEM((nslot, 3, rows, LANES), BF16),
+            pltpu.VMEM((nslot, 3, rows + 2 * HALO, LANES), BF16),
+            pltpu.VMEM((nslot, 3, rows + 2 * HALO, LANES), BF16),
+            pltpu.VMEM((rows + 2 * HALO, 16, LANES), F32),
+            pltpu.VMEM((6, rows + 2 * HALO, LANES), F32),
+            pltpu.VMEM((rows + 2 * HALO, 16, 384), BF16),
             pltpu.VMEM((tall, 16, 384), BF16),
-            pltpu.VMEM((2 * DMAX, 16, 384), BF16),
-            pltpu.VMEM((2 * DMAX, 16, 384), BF16),
             pltpu.VMEM((2, LAYERS, 3, 384, LANES), BF16),
             pltpu.VMEM((2, LAYERS, 2, 384, LANES), BF16),
             pltpu.VMEM((2, LAYERS, 9, 16, LANES), F32),
-            pltpu.VMEM((LAYERS, rows * 16, LANES), F32),
+            pltpu.VMEM((PAIRS, rows, 16, LANES), F32),
+            pltpu.VMEM((PAIRS, tall, 16, LANES), F32),
+            pltpu.VMEM((PAIRS, 2, tall, LANES), F32),
             pltpu.VMEM((rows, 16, LANES), F32),
             pltpu.VMEM((LANES, 16 * LANES), BF16),
             pltpu.VMEM((9, 48, 256), BF16),

time: 113 us -> 101 us (0.89)
  Pallas kernels: 104 us -> 94.4 us
  local copies, waits for them, and re-layouts: 7.84 us -> 5.89 us
    pallas_call x1, Pallas kernels: 104 us -> 94.4 us  [on_device(): pl.pallas_call(functools.partial(kernel, (nrow, ncol, rows, total_cells,...]
    rev x2 -> x0, local copies, waits for them, and re-layouts: 2.01 us -> none  [basis_blocks(): return windows[::-1, ::-1].reshape(9, 16, side * side)]
where the time goes in v2:
time: 101 us
  Pallas kernels  94.4 us (93%)
  local copies, waits for them, and re-layouts  5.89 us (6%)
    pallas_call x1, Pallas kernels, on_device(): pl.pallas_call(functools.partial(kernel, (nrow, ncol, rows, total_cells,...  94.4 us

profile of v2, /device:TPU:0, one launch (start us, length us, event | category | flops | bytes accessed | tf_op | source)
XLA Modules:
  0.0 101.2 jit_solution(11484512177516426346)
XLA Ops:
  0.6 1.0 pad.9
  1.6 0.6 reshape.49
  2.2 0.0 copy-start.5
  2.2 0.1 copy.26
  2.3 0.5 reshape.50.blk_ref
  2.8 0.1 copy-done.5
  2.9 0.1 copy.23
  3.0 0.1 broadcast_in_dim.17
  3.1 0.0 copy-start.3
  3.1 0.3 copy.28.target_ref
  3.5 0.4 copy-done.4
  3.8 0.3 copy.21
  4.1 0.0 copy-start.9
  4.1 0.0 copy-start.10
  4.1 0.0 copy-start.11
  4.1 0.0 copy-start.7
  4.2 0.0 copy-start.6
  4.2 0.0 copy-start
  4.2 0.0 copy-start.1
  4.2 0.0 copy-start.2
  4.2 0.3 copy.22
  4.6 0.2 copy.27.film_ref
  4.8 0.1 copy.25
  5.0 0.1 pad_maximum_fusion
  5.1 0.1 tile.9
  5.2 0.1 tile.21
  5.3 0.1 copy.30
  5.4 0.1 broadcast_in_dim.14
  5.5 0.1 broadcast_in_dim.15.active_ref
  5.6 94.4 %shard_map.140 = (f32[16,128]{1,0:T(8,128)S(1)}, f32[2,8,128]{2,1,0:T(8,128)S(1)}) custom-call(s32[4]{0:T(128)S(1)} %copy-done.2, f32[16,128]{1,0:T(8,128)S(1)} %pad.8.design_ref, f32[16,128]{1,0:T(8,128)S(1)} %broadcast_in_dim.15.active_ref, bf16[32,16,128]{2,1,0:T(8,128)(2,1)S(1)} %copy.27.film_ref, f32[32,16,128]{2,1,0:T(8,128)S(1)} %copy.28.target_ref, ...), custom_call_target="tpu_custom_call" | custom-call | tf_op jit(solution)/shard_map/pallas_call | solution.py:533
  100.0 0.7 copy.31
  100.6 0.6 slice_reduce_fusion
  (21 shorter events, 0.1 us)
Async XLA Ops:
  2.2 0.7 copy-start.5
  2.9 0.9 copy-start.4
  3.1 1.7 %copy-start.3 = (bf16[4,9,16,16]{3,2,1,0:T(8,128)(2,1)S(1)}, bf16[4,9,16,16]{3,2,1,0:T(8,128)(2,1)}, u32[]{:S(2)}) copy-start(bf16[4,9,16,16]{3,2,1,0:T(8,128)(2,1)} %param.19) | copy-start | bytes 55300
  4.1 0.9 copy-start.9
  4.1 0.9 copy-start.10
  4.1 0.9 copy-start.11
  4.1 1.0 %copy-start.7 = (f32[4,16]{1,0:T(4,128)S(1)}, f32[4,16]{1,0:T(4,128)}, u32[]{:S(2)}) copy-start(f32[4,16]{1,0:T(4,128)} %param.20) | copy-start | bytes 772
  4.2 1.1 %copy-start.6 = (f32[6,2,8]{2,1,0:T(2,128)S(1)}, f32[6,2,8]{2,1,0:T(2,128)}, u32[]{:S(2)}) copy-start(f32[6,2,8]{2,1,0:T(2,128)} %param.13) | copy-start | bytes 1156
  4.2 1.2 %copy-start.8 = (s32[2,8]{1,0:T(2,128)S(1)}, s32[2,8]{1,0:T(2,128)}, u32[]{:S(2)}) copy-start(s32[2,8]{1,0:T(2,128)} %param.14) | copy-start | bytes 196
  4.2 1.4 %copy-start = (bf16[144,144]{1,0:T(8,128)(2,1)S(1)}, bf16[144,144]{1,0:T(8,128)(2,1)}, u32[]{:S(2)}) copy-start(bf16[144,144]{1,0:T(8,128)(2,1)} %constant.7.clone.sel_ref) | copy-start | bytes 124420
  4.2 1.4 %copy-start.1 = (bf16[144,144]{1,0:T(8,128)(2,1)S(1)}, bf16[144,144]{1,0:T(8,128)(2,1)}, u32[]{:S(2)}) copy-start(bf16[144,144]{1,0:T(8,128)(2,1)} %constant.8.clone.selt_ref) | copy-start | bytes 124420
  4.2 1.3 %copy-start.2 = (s32[4]{0:T(128)S(1)}, s32[4]{0:T(128)}, u32[]{:S(2)}) copy-start(s32[4]{0:T(128)} %dil_ref.1) | copy-start | bytes 52

commit v3 on v2

--- a/solution.py
+++ b/solution.py
@@ -39,7 +39,7 @@
     dil_ref, design_ref, active_ref, film_ref, target_ref, lanes_ref, wt_ref, blk_ref, sel_ref, selt_ref,
     new_ref, obj_ref,
     edge_t, edge_b, halo_t, halo_b, edge_l, edge_r, halo_l, halo_r,
-    cf_s, side_s, xo, xn, wbig, wside, wt_s, pre_o, pre_c, pre_w, adj_s, ee_s, bfw, bbk, h_s, hd_s,
+    cf_s, side_s, xo, xn, wbig, wside, wt_s, steep_o, steep_c, steep_w, adj_s, ee_s, bfw, bbk, h_s, hd_s,
     amp9, part, got, grad9, q_s, grad_t, ar1, ar1_src, ar2, ar2_src,
     send_sem, recv_sem, ar_send, ar_recv,
 ):
@@ -183,7 +183,7 @@
                 for rx in range(3):
                     acc = jnp.where(masks[rx], wt_s[f, l, 3 * ry + rx][None], acc)
                 banded = acc.astype(BF16).reshape(384, LANES)
-                wbig[f, l, ry] = banded
+                wbig[f, l, 384 * ry : 384 * ry + 384] = banded
                 wside[f, l, 0, 128 * ry : 128 * ry + 128] = banded[0:128]
                 wside[f, l, 1, 128 * ry : 128 * ry + 128] = banded[256:384]
     ones_block = (
@@ -212,11 +212,10 @@
 
     def conv_rows(ref, f, l, at, count):
         d = dil_ref[l]
-        out = None
-        for ry in range(3):
-            lhs = ref[pl.ds(at + (ry - 1) * d, count)].reshape(16 * count, 384)
-            term = jnp.dot(lhs, wbig[f, l, ry], preferred_element_type=F32)
-            out = term if out is None else out + term
+        lhs = jnp.concatenate(
+            [ref[pl.ds(at + (ry - 1) * d, count)].reshape(16 * count, 384) for ry in range(3)], axis=1
+        )
+        out = jnp.dot(lhs, wbig[f, l], preferred_element_type=F32)
         return out.reshape(count, 16, LANES)
 
     def f32(value):
@@ -257,17 +256,18 @@
         side_s[4] = f32(halo_r[slot, 0])
         side_s[5] = f32(halo_r[slot, 1])
         d = dil_ref[l]
-        outer = None
         near = ([], [])
+        left, right = [], []
         for ry in range(3):
             six = [side_s[n, pl.ds(H - D + (ry - 1) * d, tall), :] for n in range(6)]
             for n in range(2):
                 near[n].append(six[3 * n + 1])
-            lhs = jnp.concatenate(
-                [jnp.concatenate(six[0:3], axis=1), jnp.concatenate(six[3:6], axis=1)], axis=0
-            ).astype(BF16)
-            term = jnp.dot(lhs, wbig[f, l, ry], preferred_element_type=F32)
-            outer = term if outer is None else outer + term
+            left += six[0:3]
+            right += six[3:6]
+        lhs = jnp.concatenate(
+            [jnp.concatenate(left, axis=1), jnp.concatenate(right, axis=1)], axis=0
+        ).astype(BF16)
+        outer = jnp.dot(lhs, wbig[f, l], preferred_element_type=F32)
         inner = [
             jnp.dot(
                 jnp.concatenate(near[n], axis=1).astype(BF16), wside[f, l, n], preferred_element_type=F32
@@ -293,7 +293,11 @@
         return conv_rows(xn, f, l, DMAX, rows)
 
     def sigmoid(v):
-        return 1.0 / (1.0 + jnp.exp(-v))
+        return 0.5 + 0.5 * jnp.tanh(0.5 * v)
+
+    def silu_and_slope(v):
+        s = sigmoid(v)
+        return v * s, s * (1.0 + v * (1.0 - s))
 
     def render(amp, dest):
         high, low = split2(amp.reshape(144, LANES))
@@ -334,14 +338,16 @@
             news = []
             for k in range(3):
                 pre = outs[k] + bias
+                gain, steep = silu_and_slope(pre)
                 if k == 0:
-                    pre_c[n] = pre
+                    steep_c[n] = steep
                 else:
-                    pre_w[n, k - 1] = pre
-                news.append(f32((olds[k] + pre * sigmoid(pre)).astype(BF16)))
+                    steep_w[n, k - 1] = steep
+                news.append(f32((olds[k] + gain).astype(BF16)))
             pre = near_conv(0, lb_, *news) + lanes_ref[4 + lb_ : 5 + lb_, :]
-            pre_o[n] = pre
-            state = f32((news[0][D : D + R] + pre * sigmoid(pre)).astype(BF16))
+            gain, steep = silu_and_slope(pre)
+            steep_o[n] = steep
+            state = f32((news[0][D : D + R] + gain).astype(BF16))
         pressure = None
         for piece in split2((ro * state).reshape(nx, LANES)):
             term = jnp.dot(piece, ones_block, preferred_element_type=F32)
@@ -350,14 +356,13 @@
         miss = jnp.sum(misfit * misfit, keepdims=True) * (0.5 / 16)
         adjoint = (ro * (misfit * (1.0 / 256.0))).reshape(rows, 16, LANES)
 
-        def slope_of(grad, v):
-            s = sigmoid(v)
-            return f32((grad * (s * (1.0 + v * (1.0 - s)))).astype(BF16))
+        def slope_of(grad, steep):
+            return f32((grad * steep).astype(BF16))
 
         for n in range(PAIRS):
             pair = PAIRS - 1 - n
             slot = slot0 + PAIRS + n
-            slope = slope_of(adjoint, pre_o[pair])
+            slope = slope_of(adjoint, steep_o[pair])
             outs = wide_conv(slot, base + PAIRS + n, 1, 2 * pair + 1, slope, adjoint)
             grown = jnp.concatenate(
                 [f32(halo_t[slot, HALO : HALO + D]), adjoint, f32(halo_b[slot, HALO : HALO + D])], axis=0
@@ -367,7 +372,7 @@
                 f32(halo_l[slot, 2])[D : D + tall] + outs[1],
                 f32(halo_r[slot, 2])[D : D + tall] + outs[2],
             )
-            pres = (pre_c[pair], pre_w[pair, 0], pre_w[pair, 1])
+            pres = (steep_c[pair], steep_w[pair, 0], steep_w[pair, 1])
             slopes = [slope_of(x, v) for x, v in zip(adjs, pres)]
             adjoint = adjs[0][D : D + R] + near_conv(1, 2 * pair, *slopes)
         adj_s[...] = lw * adjoint
@@ -448,7 +453,7 @@
         pltpu.make_async_copy(many, many, ar_recv.at[it, 1]).wait()
         total = jnp.sum(ar2[it], axis=0)
         scale = step_rate / jnp.sqrt(total[0:1] * (1.0 / total_entries) + norm_eps)
-        obj_ref[it] = total * (1.0 / total_cells)
+        obj_ref[it] = jnp.sum(total[1:2, 0:1]) * (1.0 / total_cells)
         new_ref[...] = new_ref[...] - gradient * scale
 
         @pl.when(more)
@@ -534,10 +539,10 @@
         functools.partial(kernel, (nrow, ncol, rows, total_cells, total_entries)),
         out_shape=(
             jax.ShapeDtypeStruct((16, LANES), F32),
-            jax.ShapeDtypeStruct((ITERS, 8, LANES), F32),
+            jax.ShapeDtypeStruct((ITERS,), F32),
         ),
         in_specs=[pl.BlockSpec(memory_space=pltpu.SMEM)] + [vmem] * 9,
-        out_specs=(vmem, vmem),
+        out_specs=(vmem, pl.BlockSpec(memory_space=pltpu.SMEM)),
         scratch_shapes=[
             pltpu.VMEM((nslot, HALO + DMAX, 16, LANES), BF16),
             pltpu.VMEM((nslot, HALO + DMAX, 16, LANES), BF16),
@@ -551,7 +556,7 @@
             pltpu.VMEM((6, rows + 2 * HALO, LANES), F32),
             pltpu.VMEM((rows + 2 * HALO, 16, 384), BF16),
             pltpu.VMEM((tall, 16, 384), BF16),
-            pltpu.VMEM((2, LAYERS, 3, 384, LANES), BF16),
+            pltpu.VMEM((2, LAYERS, 3 * 384, LANES), BF16),
             pltpu.VMEM((2, LAYERS, 2, 384, LANES), BF16),
             pltpu.VMEM((2, LAYERS, 9, 16, LANES), F32),
             pltpu.VMEM((PAIRS, rows, 16, LANES), F32),
@@ -583,7 +588,7 @@
         ),
     )(dilation, design_t, active_t, film, targ, lanes, wt, blocks, sel, sel.T)
     new_design = new[:, :nparams].T.reshape(nparams, drows, dcols)
-    return new_design, obj[:, 1, 0]
+    return new_design, obj
 
 
 def solution(mesh):

time: 101 us -> 104 us (1.030)
  Pallas kernels: 94.4 us -> 97.2 us
    pallas_call x1, Pallas kernels: 94.4 us -> 97.2 us  [on_device(): pl.pallas_call(functools.partial(kernel, (nrow, ncol, rows, total_cells,...]
where the time goes in v3:
time: 104 us
  Pallas kernels  97.2 us (93%)
  local copies, waits for them, and re-layouts  5.79 us (6%)
    pallas_call x1, Pallas kernels, on_device(): pl.pallas_call(functools.partial(kernel, (nrow, ncol, rows, total_cells,...  97.2 us

profile of v3, /device:TPU:0, one launch (start us, length us, event | category | flops | bytes accessed | tf_op | source)
XLA Modules:
  0.0 103.9 jit_solution(16856849911396197262)
XLA Ops:
  0.6 1.0 pad.9
  1.6 0.6 reshape.49
  2.2 0.0 copy-start.5
  2.2 0.1 copy.26
  2.3 0.5 reshape.50.blk_ref
  2.8 0.1 copy-done.5
  2.9 0.1 copy.23
  3.0 0.1 broadcast_in_dim.17
  3.1 0.0 copy-start.3
  3.1 0.3 copy.28.target_ref
  3.5 0.4 copy-done.4
  3.8 0.3 copy.21
  4.1 0.0 copy-start.9
  4.1 0.0 copy-start.10
  4.1 0.0 copy-start.11
  4.1 0.0 copy-start.7
  4.2 0.0 copy-start.6
  4.2 0.0 copy-start
  4.2 0.0 copy-start.1
  4.2 0.0 copy-start.2
  4.2 0.3 copy.22
  4.6 0.2 copy.27.film_ref
  4.8 0.1 copy.25
  5.0 0.1 pad_maximum_fusion
  5.1 0.1 tile.9
  5.2 0.1 tile.21
  5.3 0.1 copy.30
  5.4 0.1 broadcast_in_dim.14
  5.5 0.1 broadcast_in_dim.15.active_ref
  5.6 97.2 %shard_map.140 = (f32[16,128]{1,0:T(8,128)S(1)}, f32[2]{0:T(128)S(1)}) custom-call(s32[4]{0:T(128)S(1)} %copy-done.2, f32[16,128]{1,0:T(8,128)S(1)} %pad.8.design_ref, f32[16,128]{1,0:T(8,128)S(1)} %broadcast_in_dim.15.active_ref, bf16[32,16,128]{2,1,0:T(8,128)(2,1)S(1)} %copy.27.film_ref, f32[32,16,128]{2,1,0:T(8,128)S(1)} %copy.28.target_ref, ...), custom_call_target="tpu_custom_call" | custom-call | tf_op jit(solution)/shard_map/pallas_call | solution.py:538
  102.7 0.7 copy.31
  103.4 0.5 copy.33
  (21 shorter events, 0.1 us)
Async XLA Ops:
  2.2 0.7 copy-start.5
  2.9 0.9 copy-start.4
  3.1 1.7 %copy-start.3 = (bf16[4,9,16,16]{3,2,1,0:T(8,128)(2,1)S(1)}, bf16[4,9,16,16]{3,2,1,0:T(8,128)(2,1)}, u32[]{:S(2)}) copy-start(bf16[4,9,16,16]{3,2,1,0:T(8,128)(2,1)} %param.19) | copy-start | bytes 55300
  4.1 0.9 copy-start.9
  4.1 0.9 copy-start.10
  4.1 0.9 copy-start.11
  4.1 1.0 copy-start.7
  4.2 1.1 %copy-start.6 = (f32[6,2,8]{2,1,0:T(2,128)S(1)}, f32[6,2,8]{2,1,0:T(2,128)}, u32[]{:S(2)}) copy-start(f32[6,2,8]{2,1,0:T(2,128)} %param.13) | copy-start | bytes 1156
  4.2 1.2 %copy-start.8 = (s32[2,8]{1,0:T(2,128)S(1)}, s32[2,8]{1,0:T(2,128)}, u32[]{:S(2)}) copy-start(s32[2,8]{1,0:T(2,128)} %param.14) | copy-start | bytes 196
  4.2 1.4 %copy-start = (bf16[144,144]{1,0:T(8,128)(2,1)S(1)}, bf16[144,144]{1,0:T(8,128)(2,1)}, u32[]{:S(2)}) copy-start(bf16[144,144]{1,0:T(8,128)(2,1)} %constant.7.clone.sel_ref) | copy-start | bytes 124420
  4.2 1.4 %copy-start.1 = (bf16[144,144]{1,0:T(8,128)(2,1)S(1)}, bf16[144,144]{1,0:T(8,128)(2,1)}, u32[]{:S(2)}) copy-start(bf16[144,144]{1,0:T(8,128)(2,1)} %constant.8.clone.selt_ref) | copy-start | bytes 124420
  4.2 1.3 %copy-start.2 = (s32[4]{0:T(128)S(1)}, s32[4]{0:T(128)}, u32[]{:S(2)}) copy-start(s32[4]{0:T(128)} %dil_ref.1) | copy-start | bytes 52
